TPU v7x, 32 devices: a whole 2x2x4 slice. The times are simulated.
32 devices in a mesh: dp: 4 (over z), bank: 4 (over y, x), head: 2 (over core).
Axes of the slice: x: 2, y: 2, z: 4, core: 2. Of those that a mesh axis runs over, the one named last changes fastest.
Arguments:
- feats: bfloat16 [2048, 2048], P('dp'), may hold values from -6 to 6
- w_first: bfloat16 [2048, 2048], P(None, ('bank', 'head')), may hold values from -0.125 to 0.125
- w_second: bfloat16 [2048, 256], P(('bank', 'head')), may hold values from -0.125 to 0.125
- fresh_keys: float32 [2048, 256], P('dp'), may hold values from -6 to 6
- bank: float32 [32768, 256], P(('bank', 'head'))
- block_lists: int32 [4, 32], P('dp'), may hold values from 0 to 63, as said below
- dest_rows: int32 [2048], P('dp'), may hold values from 0 to 32767, as said below
Outputs:
- loss: float32 [2048], P('dp')
- grad_first: float32 [2048, 2048], P('dp', ('bank', 'head'))
- grad_second: float32 [2048, 256], P(('bank', 'head'))
- new_bank: float32 [32768, 256], P(('bank', 'head'))
Inputs may be any that keep to these rules, and one draw needn't show every extreme that they name: `block_lists`: each row names 32 different blocks. `dest_rows`: all entries differ; the 512 entries of query block g name exactly 64 rows in each range of rows o * 4096 to (o + 1) * 4096 - 1.
All inputs are finite; a program needn't handle non-finite values.
Results may differ from a plain program's by a relative error of at most 0.012.
Values sent between devices are 32-bit elements; how exact they have to be, the bound alone decides.
A program may use at most 128 MiB of HBM per device.

v0:
```python
import jax
import jax.numpy as jnp
from jax import lax
from jax.sharding import PartitionSpec as P

BLOCK = 512
sharpness_divisor = 0.2
epsilon = 1e-06
lowest = -1e30


def joined(array, axis, combine):
    everything = jax.tree.map(lambda part: lax.all_gather(part, axis), array)
    leading = jax.tree.map(lambda part: part[0], everything)

    def hop(k, so_far):
        return combine(so_far, jax.tree.map(lambda part: part[k], everything))

    return lax.fori_loop(1, lax.axis_size(axis), hop, leading)


def unit_rows(values):
    norms = jnp.sqrt(jnp.sum(values * values, axis=1, keepdims=True) + epsilon)
    return (values / norms, norms)


def exact_scores(anchor_matrix, bank_entries):
    return (
        lax.dot_general(
            anchor_matrix,
            bank_entries,
            (((1,), (1,)), ((), ())),
            precision=lax.Precision.HIGHEST,
            preferred_element_type=jnp.float32,
        )
        / sharpness_divisor
    )


def join_stats(first, second):
    best = jnp.maximum(first[0], second[0])
    partition_total = first[1] * jnp.exp(first[0] - best) + second[1] * jnp.exp(second[0] - best)
    return (best, partition_total)


def shards(feats, w_first, w_second, fresh_keys, bank, block_lists, dest_rows):
    owner = lax.axis_index(("bank", "head"))
    owner_rows = bank.shape[0]
    hidden = jnp.maximum(jnp.dot(feats, w_first, preferred_element_type=jnp.float32), 0.0).astype(
        jnp.bfloat16
    )
    partial_embed = jnp.dot(hidden, w_second, preferred_element_type=jnp.float32)
    embed = lax.psum(partial_embed, ("bank", "head"))
    anchor_matrix, norms = unit_rows(embed)
    unit_length_bank, unused = unit_rows(fresh_keys)
    matching_similarity = jnp.sum(anchor_matrix * unit_length_bank, axis=1) / sharpness_divisor
    listed = block_lists[0]
    blocks_here = owner_rows // BLOCK
    owned = listed // blocks_here == owner
    owned_count = jnp.sum(owned.astype(jnp.int32))
    order = jnp.argsort(jnp.where(owned, 0, 1).astype(jnp.int32), stable=True)
    local_blocks = listed[order] - owner * blocks_here
    row_count = anchor_matrix.shape[0]

    def block_keys(index):
        return lax.dynamic_slice_in_dim(bank, local_blocks[index] * BLOCK, BLOCK, 0)

    start_best = jnp.full((row_count,), lowest, jnp.float32)
    start_total = jnp.zeros((row_count,), jnp.float32)
    start_weighted = jnp.zeros((row_count, anchor_matrix.shape[1]), jnp.float32)

    def first_pass(index, carry):
        best, partition_total = carry
        similarity_matrix = exact_scores(anchor_matrix, block_keys(index))
        new_best = jnp.maximum(best, jnp.max(similarity_matrix, axis=1))
        partition_total = partition_total * jnp.exp(best - new_best) + jnp.sum(
            jnp.exp(similarity_matrix - new_best[:, None]), axis=1
        )
        return (new_best, partition_total)

    local_stats = lax.fori_loop(0, owned_count, first_pass, (start_best, start_total))
    neg_best, neg_total = joined(local_stats, ("bank", "head"), join_stats)
    best = jnp.maximum(neg_best, matching_similarity)
    positive_weight = jnp.exp(matching_similarity - best)
    partition_total = neg_total * jnp.exp(neg_best - best) + positive_weight

    def second_pass(index, probability_mixed_bank):
        bank_entries = block_keys(index)
        shares = (
            jnp.exp(exact_scores(anchor_matrix, bank_entries) - best[:, None])
            / partition_total[:, None]
        )
        return probability_mixed_bank + jnp.dot(
            shares,
            bank_entries,
            precision=lax.Precision.HIGHEST,
            preferred_element_type=jnp.float32,
        )

    local_weighted = lax.fori_loop(0, owned_count, second_pass, start_weighted)
    probability_mixed_bank = lax.psum(local_weighted, ("bank", "head"))
    loss = best + jnp.log(partition_total) - matching_similarity
    anchor_derivative = (
        probability_mixed_bank
        + (positive_weight / partition_total - 1.0)[:, None] * unit_length_bank
    ) / sharpness_divisor
    inner = jnp.sum(anchor_matrix * anchor_derivative, axis=1, keepdims=True)
    grad_z = ((anchor_derivative - anchor_matrix * inner) / norms).astype(jnp.bfloat16)
    second_part = lax.dot_general(
        hidden, grad_z, (((0,), (0,)), ((), ())), preferred_element_type=jnp.float32
    )
    grad_second = lax.psum(second_part, "dp")
    grad_hidden = lax.dot_general(
        grad_z, w_second, (((1,), (1,)), ((), ())), preferred_element_type=jnp.float32
    )
    grad_pre = jnp.where(hidden > 0, grad_hidden, 0.0).astype(jnp.bfloat16)
    grad_first = lax.psum_scatter(
        lax.dot_general(
            feats, grad_pre, (((0,), (0,)), ((), ())), preferred_element_type=jnp.float32
        ),
        "dp",
        scatter_dimension=0,
        tiled=True,
    )
    got_keys, got_dest = (
        lax.all_gather(unit_length_bank, "dp", axis=0, tiled=True),
        lax.all_gather(dest_rows.astype(jnp.float32), "dp", axis=0, tiled=True),
    )
    local_rows = got_dest.astype(jnp.int32) - owner * owner_rows
    inside = (local_rows >= 0) & (local_rows < owner_rows)
    new_bank = bank.at[jnp.where(inside, local_rows, owner_rows)].set(got_keys, mode="drop")
    return (loss, grad_first, grad_second, new_bank)


def solution(mesh):
    return jax.shard_map(
        shards,
        mesh=mesh,
        in_specs=(
            P("dp", None),
            P(None, ("bank", "head")),
            P(("bank", "head"), None),
            P("dp", None),
            P(("bank", "head"), None),
            P("dp", None),
            P("dp"),
        ),
        out_specs=(
            P("dp"),
            P("dp", ("bank", "head")),
            P(("bank", "head"), None),
            P(("bank", "head"), None),
        ),
        check_vma=False,
    )
```

profile of v0, /device:TPU:0, one launch (start us, length us, event | category | flops | bytes accessed | tf_op | source)
XLA Modules:
  0.0 383.6 jit_solution(11246029741084995186)
XLA Ops:
  7.2 4.6 %copy.49 = f32[4096,256]{1,0:T(8,128)} copy(f32[4096,256]{1,0:T(8,128)} %param.17) | data formatting | bytes 8388608
  17.1 54.1 %all-reduce.4.cloned.1.call-done = f32[512,256]{1,0:T(8,128)} async-done(((f32[512,256]{1,0:T(8,128)}), f32[512,256]{1,0:T(8,128)}) %all-reduce.4.cloned.1.call-update) | async-done | bytes 524304 | tf_op jit(solution)/shard_map/psum | solution.py:53
  74.5 36.0 %while.39 = (s32[]{:T(128)}, f32[512]{0:T(512)S(1)}, f32[512]{0:T(512)S(1)}, s32[]{:T(128)}, s32[32]{0:T(128)S(1)}, /*index=5*/f32[4096,256]{1,0:T(8,128)}, f32[...) while((s32[]{:T(128)}, f32[512]{0:T(512)S(1)}, ...), condition=%wide.region_7.8_spmd, body=%wide.region_4.0_spmd.sunk | while | flops 806355968 | bytes 3172573 | solution.py:81
  110.5 7.4 %all-gather.2 = f32[8,1,512]{2,1,0:T(1,128)S(1)} all-gather(f32[1,1,512]{2,1,0:T(1,128)S(1)} %bitcast.49), channel_id=2, replica_groups=mesh['dp'=4,'bank'=4,'head'=2] {'bank','head'}, dimensions={0}, use_global_device_ids=true | all-gather | bytes 18432 | tf_op jit(solution)/shard_map/all_gather | solution.py:13
  118.0 9.4 %all-gather.3 = f32[8,1,512]{2,1,0:T(1,128)S(1)} all-gather(f32[1,1,512]{2,1,0:T(1,128)S(1)} %bitcast.52), channel_id=3, replica_groups=mesh['dp'=4,'bank'=4,'head'=2] {'bank','head'}, dimensions={0}, use_global_device_ids=true | all-gather | bytes 18432 | tf_op jit(solution)/shard_map/all_gather | solution.py:13
  128.4 62.4 %while.41 = (s32[]{:T(128)}, f32[512,256]{1,0:T(8,128)S(1)}, s32[]{:T(128)}, s32[32]{0:T(128)}, f32[4096,256]{1,0:T(8,128)}, /*index=5*/f32[512,256]{1,0:T(8,128...) while((s32[]{:T(128)}, f32[512,256]{1,0:T(8,128)S(1)}, ...), condition=%wide.region_13.14_spmd, body=%wide.region_12.13_spmd.sunk | while | flops 1611530240 | bytes 4722921 | solution.py:100
  130.9 2.2 fusion.45
  133.1 3.0 convolution_add_fusion.2
  140.8 3.0 convolution_add_fusion.2
  148.5 3.0 convolution_add_fusion.2
  154.1 2.2 fusion.45
  156.3 3.0 convolution_add_fusion.2
  164.0 3.0 convolution_add_fusion.2
  169.5 2.2 fusion.45
  171.7 3.0 convolution_add_fusion.2
  179.4 3.0 convolution_add_fusion.2
  187.1 3.0 convolution_add_fusion.2
  192.4 52.9 %all-reduce.6.cloned.1.call-done = f32[512,256]{1,0:T(8,128)} async-done(((f32[512,256]{1,0:T(8,128)}), f32[512,256]{1,0:T(8,128)}) %all-reduce.6.cloned.1.call-update) | async-done | bytes 524304 | tf_op jit(solution)/shard_map/psum | solution.py:101
  248.8 3.3 convolution_bitcast_fusion
  252.8 12.1 %all-gather.4 = f32[4,1,512]{2,1,0:T(1,128)S(1)} all-gather(f32[1,1,512]{2,1,0:T(1,128)S(1)} %bitcast.58), channel_id=1, replica_groups=mesh['dp'=4,'bank'=4,'head'=2] {'dp'}, dimensions={0}, use_global_device_ids=true | all-gather | bytes 10240 | tf_op jit(solution)/shard_map/all_gather | solution.py:127
  265.9 27.0 %all-gather.7.cloned.1.call-done = f32[2048,256]{1,0:T(8,128)} async-done(((f32[512,256]{1,0:T(8,128)}), f32[2048,256]{1,0:T(8,128)}) %all-gather.7.cloned.1.call-update) | async-done | bytes 2097168 | tf_op jit(solution)/shard_map/all_gather | solution.py:126
  292.9 13.6 %scatter_fusion = f32[4096,256]{1,0:T(8,128)} fusion(f32[4096,256]{1,0:T(8,128)} %get-tuple-element.541, s32[2048]{0:T(1024)S(1)} %compare_select_fusion, f32[2048,256]{1,0:T(8,128)} %all-gather.7.cloned.1.call-done), kind=kCustom, calls=%fused_computation.1 | custom fusion | bytes 6299648 | tf_op jit(solution)/shard_map/scatter | solution.py:131
  306.5 31.3 %reduce-scatter.2.cloned.1.call-done = f32[512,256]{0,1:T(8,128)} async-done(((f32[2048,256]{0,1:T(8,128)}), f32[512,256]{0,1:T(8,128)}) %reduce-scatter.2.cloned.1.call-update) | async-done | bytes 524304 | tf_op jit(solution)/shard_map/reduce_scatter | solution.py:117
  339.9 35.6 %all-reduce.8.cloned.1.call-done = f32[256,256]{1,0:T(8,128)} async-done(((f32[256,256]{1,0:T(8,128)}), f32[256,256]{1,0:T(8,128)}) %all-reduce.8.cloned.1.call-update) | async-done | bytes 262160 | tf_op jit(solution)/shard_map/psum | solution.py:112
  (136 shorter events, 65.0 us)
Async XLA Ops:
  7.2 4.7 %copy-start = (bf16[512,2048]{1,0:T(8,128)(2,1)S(1)}, bf16[512,2048]{1,0:T(8,128)(2,1)}, u32[]{:S(2)}) copy-start(bf16[512,2048]{1,0:T(8,128)(2,1)} %param.13) | copy-start | bytes 6291460
  7.2 64.1 %all-reduce.4.cloned.1.call-start = ((), (), s32[]{:S(2)}) async-start(), calls=%async_computation.1 | async-start | bytes 1048576 | tf_op jit(solution)/shard_map/psum | solution.py:53
  7.2 4.6 %copy-start.9 = (bf16[2048,256]{1,0:T(8,128)(2,1)S(1)}, bf16[2048,256]{1,0:T(8,128)(2,1)}, u32[]{:S(2)}) copy-start(bf16[2048,256]{1,0:T(8,128)(2,1)} %param.14) | copy-start | bytes 3145732
  11.9 0.9 copy-start.6
  11.9 2.0 copy-start.1
  11.9 5.1 %copy-start.5 = (f32[512,256]{1,0:T(8,128)S(1)}, f32[512,256]{1,0:T(8,128)}, u32[]{:S(2)}) copy-start(f32[512,256]{1,0:T(8,128)} %param.16) | copy-start | bytes 1572868
  13.8 231.5 %all-reduce.6.cloned.1.call-start = ((), (), s32[]{:S(2)}) async-start(), calls=%async_computation.2 | async-start | bytes 1048576 | tf_op jit(solution)/shard_map/psum | solution.py:101
  110.5 17.2 %copy-start.8 = (s32[32]{0:T(128)}, s32[32]{0:T(128)S(1)}, u32[]{:S(2)}) copy-start(s32[32]{0:T(128)S(1)} %get-tuple-element.559) | copy-start | bytes 388
  190.8 0.8 copy-start.2
  191.6 55.2 %copy-start.3 = (f32[512,256]{1,0:T(8,128)S(1)}, f32[512,256]{1,0:T(8,128)}, u32[]{:S(2)}) copy-start(f32[512,256]{1,0:T(8,128)} %get-tuple-element.283) | copy-start | bytes 1572868
  191.6 101.3 %all-gather.7.cloned.1.call-start = ((), (), s32[]{:S(2)}) async-start(), calls=%async_computation.5 | async-start | bytes 2621440 | tf_op jit(solution)/shard_map/all_gather | solution.py:126
  192.4 145.5 %reduce-scatter.2.cloned.1.call-start = ((), (), s32[]{:S(2)}) async-start(), calls=%async_computation.3 | async-start | bytes 2621440 | tf_op jit(solution)/shard_map/reduce_scatter | solution.py:117
  252.1 0.7 copy-start.7
  252.1 12.8 %copy-start.4 = (bf16[512,256]{1,0:T(8,128)(2,1)S(1)}, bf16[512,256]{1,0:T(8,128)(2,1)}, u32[]{:S(2)}) copy-start(bf16[512,256]{1,0:T(8,128)(2,1)} %divide_convert_fusion) | copy-start | bytes 786436
  252.2 123.3 %all-reduce.8.cloned.1.call-start = ((), (), s32[]{:S(2)}) async-start(), calls=%async_computation.4 | async-start | bytes 524288 | tf_op jit(solution)/shard_map/psum | solution.py:112
Sparse Core Ops, SparseCore 0:
  13.9 57.2 all-reduce.3
  191.8 53.5 all-reduce.5
  247.5 45.3 all-gather.6
  295.1 42.7 reduce-scatter.1
  340.7 34.6 all-reduce.7
where the time goes:
time: 386 us; the launch traced here: 384 us
  waiting for transfers between devices  202 us (52%)
  matrix products  64.2 us (17%)
  local copies, waits for them, and re-layouts  39.8 us (10%)
  blocking collectives  28.9 us (7%)
  loops' own time  23.3 us (6%)
  between operations  14 us (4%)
  other arithmetic  11.7 us (3%)
    psum x1, waiting for transfers between devices, shards(): embed = lax.psum(partial_embed, ('bank', 'head'))  54.1 us
    psum x1, waiting for transfers between devices, shards(): probability_mixed_bank = lax.psum(local_weighted, ('bank', 'head'))  52.9 us
    psum x1, waiting for transfers between devices, shards(): grad_second = lax.psum(second_part, 'dp')  35.6 us
    dot_general x16, matrix products, exact_scores(): lax.dot_general(anchor_matrix, bank_entries, (((1,), (1,)), ((), ())), pr...  34.4 us
    reduce_scatter x1, waiting for transfers between devices, shards(): lax.psum_scatter(lax.dot_general(feats, grad_pre, (((0,), (0,)), ((), ())...  31.3 us
    all_gather x1, waiting for transfers between devices, shards(): lax.all_gather(unit_length_bank, 'dp', axis=0, tiled=True)  27 us
    dot_general x8, matrix products, second_pass(): jnp.dot(shares, bank_entries, precision=lax.Precision.HIGHEST, preferred_...  23.8 us
    all_gather x2, blocking collectives, joined(): everything = jax.tree.map(lambda part: lax.all_gather(part, axis), array)  16.8 us
  transfers between devices with their start and end apart: 5, of which 5 were waited for; matrix products, arithmetic and copies ran while one was open for 7% of the time, Pallas kernels for 0%

commit v1 on v0

--- a/solution.py
+++ b/solution.py
@@ -7,6 +7,19 @@
 sharpness_divisor = 0.2
 epsilon = 1e-06
 lowest = -1e30
+
+
+def collect(shard, axis, dim):
+    ways = lax.axis_size(axis)
+    up = [(d, (d + 1) % ways) for d in range(ways)]
+    down = [(d, (d - 1) % ways) for d in range(ways)]
+    earlier, later = ([shard], [shard])
+    for _ in range(ways // 2):
+        earlier.append(lax.ppermute(earlier[-1], axis, up))
+    for _ in range((ways - 1) // 2):
+        later.append(lax.ppermute(later[-1], axis, down))
+    line = jnp.concatenate([*earlier[::-1], *later[1:]], axis=dim)
+    return jnp.roll(line, (lax.axis_index(axis) - ways // 2) * shard.shape[dim], axis=dim)
 
 
 def joined(array, axis, combine):
@@ -123,7 +136,7 @@
         tiled=True,
     )
     got_keys, got_dest = (
-        lax.all_gather(unit_length_bank, "dp", axis=0, tiled=True),
+        collect(unit_length_bank, "dp", 0),
         lax.all_gather(dest_rows.astype(jnp.float32), "dp", axis=0, tiled=True),
     )
     local_rows = got_dest.astype(jnp.int32) - owner * owner_rows

time: 386 us -> 357 us (0.925)
  waiting for transfers between devices: 202 us -> 160 us
  local copies, waits for them, and re-layouts: 39.8 us -> 51.8 us
    all_gather x1 -> x0, waiting for transfers between devices: 27 us -> none  [shards(): lax.all_gather(unit_length_bank, 'dp', axis=0, tiled=True)]
    reduce_scatter x1, waiting for transfers between devices: 31.3 us -> 14.9 us  [shards(): lax.psum_scatter(lax.dot_general(feats, grad_pre, (((0,), (0,)), ((), ())...]
    ppermute x0 -> x3, waiting for transfers between devices: none -> 12.1 us  [the longest x2 12.1 us: collect(): earlier.append(lax.ppermute(earlier[-1], axis, up))]
    unnamed x25 -> x27, local copies, waits for them, and re-layouts: 9.96 us -> 20.5 us
    psum x1, waiting for transfers between devices: 52.9 us -> 42.9 us  [shards(): probability_mixed_bank = lax.psum(local_weighted, ('bank', 'head'))]
  transfers between devices with their start and end apart: 5 -> 7, of which waited for: 5 -> 5; matrix products, arithmetic and copies ran while one was open for 7% -> 24% of each run, Pallas kernels for 0% -> 0%
where the time goes in v1:
time: 357 us; the launch traced here: 355 us
  waiting for transfers between devices  160 us (45%)
  matrix products  63.2 us (18%)
  local copies, waits for them, and re-layouts  51.8 us (15%)
  blocking collectives  28.9 us (8%)
  loops' own time  21.9 us (6%)
  between operations  14 us (4%)
  other arithmetic  11.7 us (3%)
  starting transfers between devices  4.01 us (1%)
    psum x1, waiting for transfers between devices, shards(): embed = lax.psum(partial_embed, ('bank', 'head'))  54.2 us
    psum x1, waiting for transfers between devices, shards(): probability_mixed_bank = lax.psum(local_weighted, ('bank', 'head'))  42.9 us
    psum x1, waiting for transfers between devices, shards(): grad_second = lax.psum(second_part, 'dp')  35.6 us
    dot_general x16, matrix products, exact_scores(): lax.dot_general(anchor_matrix, bank_entries, (((1,), (1,)), ((), ())), pr...  34.4 us
    dot_general x8, matrix products, second_pass(): jnp.dot(shares, bank_entries, precision=lax.Precision.HIGHEST, preferred_...  23.8 us
    unnamed x27, local copies, waits for them, and re-layouts  20.5 us
    all_gather x2, blocking collectives, joined(): everything = jax.tree.map(lambda part: lax.all_gather(part, axis), array)  16.8 us
    dynamic_slice x16, local copies, waits for them, and re-layouts, block_keys(): return lax.dynamic_slice_in_dim(bank, local_blocks[index] * BLOCK, BLOCK, 0)  15.2 us
  transfers between devices with their start and end apart: 7, of which 5 were waited for; matrix products, arithmetic and copies ran while one was open for 24% of the time, Pallas kernels for 0%

profile of v1, /device:TPU:0, one launch (start us, length us, event | category | flops | bytes accessed | tf_op | source)
XLA Modules:
  0.0 355.2 jit_solution(13630992827867676711)
XLA Ops:
  7.2 4.6 %copy.56 = f32[4096,256]{1,0:T(8,128)} copy(f32[4096,256]{1,0:T(8,128)} %param.17) | data formatting | bytes 8388608
  16.9 54.2 %all-reduce.4.cloned.1.call-done = f32[512,256]{1,0:T(8,128)} async-done(((f32[512,256]{1,0:T(8,128)}), f32[512,256]{1,0:T(8,128)}) %all-reduce.4.cloned.1.call-update) | async-done | bytes 524304 | tf_op jit(solution)/shard_map/psum | solution.py:66
  74.3 34.9 %while.39 = (s32[]{:T(128)}, f32[512]{0:T(512)S(1)}, f32[512]{0:T(512)S(1)}, s32[]{:T(128)}, s32[32]{0:T(128)S(1)}, /*index=5*/f32[4096,256]{1,0:T(8,128)}, f32[...) while((s32[]{:T(128)}, f32[512]{0:T(512)S(1)}, ...), condition=%wide.region_7.8_spmd, body=%wide.region_4.0_spmd.sunk | while | flops 806355968 | bytes 3172573 | solution.py:94
  109.3 7.4 %all-gather.2 = f32[8,1,512]{2,1,0:T(1,128)S(1)} all-gather(f32[1,1,512]{2,1,0:T(1,128)S(1)} %bitcast.48), channel_id=2, replica_groups=mesh['dp'=4,'bank'=4,'head'=2] {'bank','head'}, dimensions={0}, use_global_device_ids=true | all-gather | bytes 18432 | tf_op jit(solution)/shard_map/all_gather | solution.py:26
  116.7 9.4 %all-gather.3 = f32[8,1,512]{2,1,0:T(1,128)S(1)} all-gather(f32[1,1,512]{2,1,0:T(1,128)S(1)} %bitcast.51), channel_id=3, replica_groups=mesh['dp'=4,'bank'=4,'head'=2] {'bank','head'}, dimensions={0}, use_global_device_ids=true | all-gather | bytes 18432 | tf_op jit(solution)/shard_map/all_gather | solution.py:26
  127.5 2.4 collective-permute-start.2
  130.9 12.1 %collective-permute-done = f32[512,256]{1,0:T(8,128)} collective-permute-done((f32[512,256]{1,0:T(8,128)}, f32[512,256]{1,0:T(8,128)}, u32[]{:S(2)}, u32[]{:S(2)}) %collective-permute-start) | collective-permute-done | bytes 524320 | tf_op jit(solution)/shard_map/ppermute | solution.py:18
  143.1 61.9 %while.41 = (s32[]{:T(128)}, f32[512,256]{1,0:T(8,128)S(1)}, s32[]{:T(128)}, s32[32]{0:T(128)}, f32[4096,256]{1,0:T(8,128)}, /*index=5*/f32[512,256]{1,0:T(8,128...) while((s32[]{:T(128)}, f32[512,256]{1,0:T(8,128)S(1)}, ...), condition=%wide.region_13.14_spmd, body=%wide.region_12.13_spmd.sunk | while | flops 1611530240 | bytes 4722921 | solution.py:113
  147.7 3.0 convolution_add_fusion.2
  155.4 3.0 convolution_add_fusion.2
  160.9 2.2 fusion.47
  163.1 3.0 convolution_add_fusion.2
  170.7 3.0 convolution_add_fusion.2
  176.2 2.2 fusion.47
  178.4 3.0 convolution_add_fusion.2
  186.0 3.0 convolution_add_fusion.2
  193.7 3.0 convolution_add_fusion.2
  201.3 3.0 convolution_add_fusion.2
  217.1 42.9 %all-reduce.6.cloned.1.call-done = f32[512,256]{1,0:T(8,128)} async-done(((f32[512,256]{1,0:T(8,128)}), f32[512,256]{1,0:T(8,128)}) %all-reduce.6.cloned.1.call-update) | async-done | bytes 524304 | tf_op jit(solution)/shard_map/psum | solution.py:114
  263.6 2.4 convolution_bitcast_fusion
  266.1 12.1 %all-gather.4 = f32[4,1,512]{2,1,0:T(1,128)S(1)} all-gather(f32[1,1,512]{2,1,0:T(1,128)S(1)} %bitcast.57), channel_id=1, replica_groups=mesh['dp'=4,'bank'=4,'head'=2] {'dp'}, dimensions={0}, use_global_device_ids=true | all-gather | bytes 10240 | tf_op jit(solution)/shard_map/all_gather | solution.py:140
  281.1 13.4 %scatter_custom_fusion = f32[4096,256]{1,0:T(8,128)} fusion(f32[4096,256]{1,0:T(8,128)} %get-tuple-element.546, s32[2048]{0:T(1024)S(1)} %compare_select_fusion, f32[4096,256]{1,0:T(8,128)} %constant_dynamic-update-slice_fusion, s32[]{:T(128)S(6)} %select_n.66, s32[]{:T(128)} %constant.127.clone.1), kind=kCustom, calls=%fused_computation.20 | custom fusion | bytes 6291972 | tf_op jit(solution)/shard_map/scatter | solution.py:144
  294.5 14.9 %reduce-scatter.2.cloned.1.call-done = f32[512,256]{0,1:T(8,128)} async-done(((f32[2048,256]{0,1:T(8,128)}), f32[512,256]{0,1:T(8,128)}) %reduce-scatter.2.cloned.1.call-update) | async-done | bytes 524304 | tf_op jit(solution)/shard_map/reduce_scatter | solution.py:130
  311.4 35.6 %all-reduce.8.cloned.1.call-done = f32[256,256]{1,0:T(8,128)} async-done(((f32[256,256]{1,0:T(8,128)}), f32[256,256]{1,0:T(8,128)}) %all-reduce.8.cloned.1.call-update) | async-done | bytes 262160 | tf_op jit(solution)/shard_map/psum | solution.py:125
  (142 shorter events, 80.2 us)
Async XLA Ops:
  7.2 4.7 %copy-start = (bf16[512,2048]{1,0:T(8,128)(2,1)S(1)}, bf16[512,2048]{1,0:T(8,128)(2,1)}, u32[]{:S(2)}) copy-start(bf16[512,2048]{1,0:T(8,128)(2,1)} %param.13) | copy-start | bytes 6291460
  7.2 5.4 %copy-start.4 = (bf16[256,256]{1,0:T(8,128)(2,1)S(1)}, bf16[256,256]{1,0:T(8,128)(2,1)}, u32[]{:S(2)}) copy-start(bf16[256,256]{1,0:T(8,128)(2,1)} %param.15) | copy-start | bytes 393220
  7.2 63.9 %all-reduce.4.cloned.1.call-start = ((), (), s32[]{:S(2)}) async-start(), calls=%async_computation.1 | async-start | bytes 1048576 | tf_op jit(solution)/shard_map/psum | solution.py:66
  7.2 4.6 %copy-start.7 = (bf16[2048,256]{1,0:T(8,128)(2,1)S(1)}, bf16[2048,256]{1,0:T(8,128)(2,1)}, u32[]{:S(2)}) copy-start(bf16[2048,256]{1,0:T(8,128)(2,1)} %param.14) | copy-start | bytes 3145732
  11.9 1.8 copy-start.1
  11.9 4.9 %copy-start.3 = (f32[512,256]{1,0:T(8,128)S(1)}, f32[512,256]{1,0:T(8,128)}, u32[]{:S(2)}) copy-start(f32[512,256]{1,0:T(8,128)} %param.16) | copy-start | bytes 1572868
  13.7 246.4 %all-reduce.6.cloned.1.call-start = ((), (), s32[]{:S(2)}) async-start(), calls=%async_computation.2 | async-start | bytes 1048576 | tf_op jit(solution)/shard_map/psum | solution.py:114
  109.3 21.0 %copy-start.6 = (s32[32]{0:T(128)}, s32[32]{0:T(128)S(1)}, u32[]{:S(2)}) copy-start(s32[32]{0:T(128)S(1)} %get-tuple-element.557) | copy-start | bytes 388
  126.1 16.9 %collective-permute-start = (f32[512,256]{1,0:T(8,128)}, f32[512,256]{1,0:T(8,128)}, u32[]{:S(2)}, u32[]{:S(2)}) collective-permute-start(f32[512,256]{1,0:T(8,128)} %get-tuple-element.283), channel_id=1, source_target_pairs={{0,8},{8,16},{16,24},{24,0},{1,9},{9,17},{17,25},{25,1},{2,10},{10... | collective-permute-start | bytes 1572872 | tf_op jit(solution)/shard_map/ppermute | solution.py:18
  127.5 84.0 %collective-permute-start.2 = (f32[512,256]{1,0:T(8,128)}, f32[512,256]{1,0:T(8,128)}, u32[]{:S(2)}, u32[]{:S(2)}) collective-permute-start(f32[512,256]{1,0:T(8,128)} %get-tuple-element.283), channel_id=1, source_target_pairs={{0,24},{8,0},{16,8},{24,16},{1,25},{9,1},{17,9},{25,17},{2,26},{10... | collective-permute-start | bytes 1572872 | tf_op jit(solution)/shard_map/ppermute | solution.py:20
  143.0 62.8 %collective-permute-start.1 = (f32[512,256]{1,0:T(8,128)}, f32[512,256]{1,0:T(8,128)}, u32[]{:S(2)}, u32[]{:S(2)}) collective-permute-start(f32[512,256]{1,0:T(8,128)} %collective-permute-done), channel_id=1, source_target_pairs={{0,8},{8,16},{16,24},{24,0},{1,9},{9,17},{17,25},{25,1},{2,10},{10... | collective-permute-start | bytes 1572872 | tf_op jit(solution)/shard_map/ppermute | solution.py:18
  205.0 0.8 copy-start.2
  205.8 103.6 %reduce-scatter.2.cloned.1.call-start = ((), (), s32[]{:S(2)}) async-start(), calls=%async_computation.3 | async-start | bytes 2621440 | tf_op jit(solution)/shard_map/reduce_scatter | solution.py:130
  262.1 4.0 %copy-start.5 = (s32[512]{0:T(512)S(1)}, s32[512]{0:T(512)}, u32[]{:S(2)}) copy-start(s32[512]{0:T(512)} %param.19) | copy-start | bytes 6148
  266.0 81.0 %all-reduce.8.cloned.1.call-start = ((), (), s32[]{:S(2)}) async-start(), calls=%async_computation.4 | async-start | bytes 524288 | tf_op jit(solution)/shard_map/psum | solution.py:125
Sparse Core Ops, SparseCore 0:
  13.8 57.2 all-reduce.3
  205.9 54.0 all-reduce.5
  266.2 43.1 reduce-scatter.1
  312.3 34.6 all-reduce.7
